TPU v7x, 512 devices: a whole 4x4x16 slice. The times are simulated.
512 devices in a mesh: row: 32 (over x, y, core), col: 16 (over z).
Axes of the slice: x: 4, y: 4, z: 16, core: 2. Of those that a mesh axis runs over, the one named last changes fastest.
Arguments:
- diag_factor: float32 [1024, 1024], P('row', 'col'), may hold values from -1 to 2.5, as said below
- panel_factor: float32 [16384, 1024], P('row', 'col'), may hold values from -0.046875 to 0.046875
- left_factor: float32 [16384, 8192], P('row', 'col'), may hold values from -0.046875 to 0.046875
- pivot_factor: float32 [1024, 8192], P('row', 'col'), may hold values from -0.1875 to 0.1875
- panel_adjoint: float32 [16384, 1024], P('row', 'col'), may hold values from -6 to 6
- left_adjoint: float32 [16384, 8192], P('row', 'col'), may hold values from -6 to 6
- pivot_adjoint: float32 [1024, 8192], P('row', 'col'), may hold values from -6 to 6
- diag_adjoint: float32 [1024, 1024], P('row', 'col'), may hold values from -6 to 6
Outputs:
- solved_panel: float32 [16384, 1024], P('row', 'col')
- left_out: float32 [16384, 8192], P('row', 'col')
- pivot_out: float32 [1024, 8192], P('row', 'col')
- diag_out: float32 [1024, 1024], P('row', 'col')
Inputs may be any that keep to these rules, and one draw needn't show every extreme that they name: diag_factor is lower triangular: zero above the diagonal, diagonal entries at least 1.
All inputs are finite; a program needn't handle non-finite values.
Results may differ from a plain program's by a relative error of at most 0.000073.
Values sent between devices are 32-bit elements; how exact they have to be, the bound alone decides.
A program may use at most 64 MiB of HBM per device.

v0:
```python
import jax
import jax.numpy as jnp
from jax import lax
from jax.sharding import PartitionSpec as P


def right_solve(tile, source):
    return jax.scipy.linalg.solve_triangular(tile, source.T, trans="T", lower=True).T


def local(
    diag_factor,
    panel_factor,
    left_factor,
    pivot_factor,
    panel_adjoint,
    left_adjoint,
    pivot_adjoint,
    diag_adjoint,
):
    highest = lax.Precision.HIGHEST
    block_width = panel_adjoint.shape[1]
    my_col = lax.axis_index("col")
    my_row = lax.axis_index("row")
    column_block = lax.all_gather(diag_factor, "row", axis=0, tiled=True)
    whole_diag = lax.all_gather(column_block, "col", axis=1, tiled=True)
    full_rows = lax.all_gather(panel_adjoint, "col", axis=1, tiled=True)
    solved = right_solve(whole_diag, full_rows)
    solved_panel = lax.dynamic_slice_in_dim(solved, my_col * block_width, block_width, 1)
    picked = solved
    left_out = left_adjoint - jnp.dot(
        picked,
        lax.all_gather(pivot_factor, "row", axis=0, tiled=True),
        precision=highest,
        preferred_element_type=jnp.float32,
    )
    own_rows = diag_adjoint.shape[0]
    picked = solved
    pivot_sum = lax.psum_scatter(
        jnp.einsum("rk,rc->kc", picked, left_factor, precision=highest),
        "row",
        scatter_dimension=0,
        tiled=True,
    )
    picked = solved
    square_sum = lax.psum_scatter(
        jnp.einsum("rk,rc->kc", picked, panel_factor, precision=highest),
        "row",
        scatter_dimension=0,
        tiled=True,
    )
    pivot_out = pivot_adjoint - pivot_sum
    global_row = my_row * own_rows + lax.broadcasted_iota(jnp.int32, (own_rows, block_width), 0)
    global_col = my_col * block_width + lax.broadcasted_iota(jnp.int32, (own_rows, block_width), 1)
    diag_out = diag_adjoint - jnp.where(global_col <= global_row, square_sum, 0.0)
    return (solved_panel, left_out, pivot_out, diag_out)


def solution(mesh):
    in_specs = (
        P("row", "col"),
        P("row", "col"),
        P("row", "col"),
        P("row", "col"),
        P("row", "col"),
        P("row", "col"),
        P("row", "col"),
        P("row", "col"),
    )
    out_specs = (P("row", "col"), P("row", "col"), P("row", "col"), P("row", "col"))
    return jax.shard_map(local, mesh=mesh, in_specs=in_specs, out_specs=out_specs, check_vma=False)
```

profile of v0, /device:TPU:2, one launch (start us, length us, event | category | flops | bytes accessed | tf_op | source)
XLA Modules:
  0.0 463.6 jit_solution(8965409141635587499)
XLA Ops:
  7.2 27.8 %all_gather.12 = f32[1024,64]{1,0:T(8,128)S(1)} all-gather(f32[32,64]{1,0:T(8,128)} %param.8), channel_id=1, replica_groups=mesh['row'=32,'col'=16] {'row'}, dimensions={0}, use_global_device_ids=true | all-gather | bytes 270336 | tf_op jit(solution)/shard_map/all_gather | solution.py:25
  35.0 0.9 copy.14
  36.0 0.7 all-gather.6.cloned.1.call-update
  36.7 0.7 all-gather.8.cloned.1.call-update
  37.5 77.2 %all-gather.4.cloned.1.call-done = f32[1024,1024]{0,1:T(8,128)} async-done(((f32[1024,64]{0,1:T(8,128)}), f32[1024,1024]{0,1:T(8,128)}) %all-gather.4.cloned.1.call-update) | async-done | bytes 4194320 | tf_op jit(solution)/shard_map/all_gather | solution.py:26
  114.7 4.8 %fusion = f32[1024,1024]{0,1:T(8,128)} fusion(f32[1024,1024]{0,1:T(8,128)} %all-gather.4.cloned.1.call-done), kind=kLoop, calls=%fused_computation.3 | loop fusion | flops 2097152 | bytes 8388608 | tf_op jit(solution)/shard_map/jit(_solve_triangular)/triangular_solve | solution.py:8
  119.5 24.1 %while.1 = (s32[]{:T(128)}, f32[1024,1024]{0,1:T(8,128)}, s32[8,2]{0,1:T(2,128)S(1)}, f32[8,128,128]{2,1,0:T(8,128)S(1)}, s32[]{:T(128)}) while((s32[]{:T(128)}, f32[1024,1024]{0,1:T(8,128)}, s32[8,2]{0,1:T(2,128)S(1)}, f32[8,128,128]{2,1,0:T(8,128)S(1)}, s32[]{:T(128)}) %tuple.28), condition=%wide.while_cond, body=%wide.while_body.sunk | while | flops 2 | bytes 393321 | solution.py:8
  119.5 0.5 fusion.55
  120.1 2.3 dynamic-slice.12
  122.6 0.5 fusion.55
  123.1 2.3 dynamic-slice.12
  125.6 0.5 fusion.55
  126.1 2.3 dynamic-slice.12
  128.6 0.5 fusion.55
  129.1 2.3 dynamic-slice.12
  131.6 0.5 fusion.55
  132.2 2.3 dynamic-slice.12
  134.7 0.5 fusion.55
  135.2 2.3 dynamic-slice.12
  137.7 0.5 fusion.55
  138.2 2.3 dynamic-slice.12
  140.7 0.5 fusion.55
  141.2 2.2 dynamic-slice.12
  143.6 78.6 %custom-call.4 = f32[8,128,128]{1,2,0:T(8,128)S(1)} custom-call(f32[8,128,128]{2,1,0:T(8,128)S(1)} %get-tuple-element.11), custom_call_target="InvertDiagBlocksLowerTriangular" | custom-call | tf_op jit(solution)/shard_map/jit(_solve_triangular)/triangular_solve | solution.py:8
  222.2 1.5 fusion.19
  223.8 1.4 convolution_subtract_fusion.4
  225.1 0.4 fusion.25
  225.5 1.4 convolution_subtract_fusion.3
  227.0 0.4 fusion.26
  227.3 1.6 convolution_subtract_fusion.6
  228.9 0.4 fusion.27
  229.3 1.7 convolution_subtract_fusion.7
  230.9 0.4 constant_dynamic-update-slice_fusion.4
  231.4 1.9 convolution_subtract_fusion.2
  233.3 0.4 constant_dynamic-update-slice_fusion.10
  233.8 2.0 convolution_subtract_fusion.5
  235.9 0.4 constant_dynamic-update-slice_fusion.17
  236.4 2.2 convolution_subtract_fusion.1
  238.6 1.2 convolution_dynamic-update-slice_fusion
  240.1 2.6 fusion.36
  242.7 0.3 reduce-scatter.3.cloned.1.call-start
  243.0 4.8 %fusion.35 = f32[1024,512]{1,0:T(8,128)} fusion(f32[1024,512]{1,0:T(8,128)S(1)} %constant_dynamic-update-slice_fusion.18, f32[512,512]{1,0:T(8,128)S(1)} %copy-done), kind=kOutput, calls=%fused_computation.85 | convolution fusion | flops 3221225472 | bytes 5242880 | tf_op jit(solution)/shard_map/rk,rc->kc/dot_general | solution.py:40
  247.8 0.7 dynamic-slice_bitcast_fusion
  248.5 6.3 %convolution_subtract_fusion = f32[512,512]{1,0:T(8,128)} fusion(f32[512,512]{1,0:T(8,128)} %param.13, f32[1024,512]{1,0:T(8,128)S(1)} %constant_dynamic-update-slice_fusion.18, f32[1024,512]{1,0:T(8,128)} %all-gather.8.cloned.1.call-done), kind=kOutput, calls=%fused_computation.4 | convolution fusion | flops 3221487616 | bytes 6291456 | tf_op jit(solution)/shard_map/dot_general | solution.py:31
  254.9 95.1 %reduce-scatter.5.cloned.1.call-done = f32[32,64]{1,0:T(8,128)} async-done(((f32[1024,64]{1,0:T(8,128)}), f32[32,64]{1,0:T(8,128)}) %reduce-scatter.5.cloned.1.call-update) | async-done | bytes 8208 | tf_op jit(solution)/shard_map/reduce_scatter | solution.py:46
  349.9 1.4 select_subtract_fusion
  351.3 104.3 %reduce-scatter.3.cloned.1.call-done = f32[32,512]{1,0:T(8,128)} async-done(((f32[1024,512]{1,0:T(8,128)}), f32[32,512]{1,0:T(8,128)}) %reduce-scatter.3.cloned.1.call-update) | async-done | bytes 65552 | tf_op jit(solution)/shard_map/reduce_scatter | solution.py:39
  455.6 1.5 sub.10
  (72 shorter events, 2.1 us)
Async XLA Ops:
  7.2 235.8 %copy-start = (f32[512,512]{1,0:T(8,128)S(1)}, f32[512,512]{1,0:T(8,128)}, u32[]{:S(2)}) copy-start(f32[512,512]{1,0:T(8,128)} %param.10) | copy-start | bytes 3145732
  7.2 107.5 %all-gather.4.cloned.1.call-start = ((), (), s32[]{:S(2)}) async-start(), calls=%async_computation.2 | async-start | bytes 4456448 | tf_op jit(solution)/shard_map/all_gather | solution.py:26
  35.9 186.3 %all-gather.6.cloned.1.call-start = ((), (), s32[]{:S(2)}) async-start(), calls=%async_computation.3 | async-start | bytes 2228224 | tf_op jit(solution)/shard_map/all_gather | solution.py:27
  36.7 211.8 %all-gather.8.cloned.1.call-start = ((), (), s32[]{:S(2)}) async-start(), calls=%async_computation.4 | async-start | bytes 2162688 | tf_op jit(solution)/shard_map/all_gather | solution.py:33
  37.4 312.5 %reduce-scatter.5.cloned.1.call-start = ((), (), s32[]{:S(2)}) async-start(), calls=%async_computation.6 | async-start | bytes 540672 | tf_op jit(solution)/shard_map/reduce_scatter | solution.py:46
  222.2 13.7 %copy-start.2 = (f32[8,128,128]{1,2,0:T(8,128)}, f32[8,128,128]{1,2,0:T(8,128)S(1)}, u32[]{:S(2)}) copy-start(f32[8,128,128]{1,2,0:T(8,128)S(1)} %custom-call.4) | copy-start | bytes 1572868
  222.2 5.1 %copy-start.1 = (f32[512,1024]{0,1:T(8,128)S(1)}, f32[512,1024]{0,1:T(8,128)}, u32[]{:S(2)}) copy-start(f32[512,1024]{0,1:T(8,128)} %all-gather.6.cloned.1.call-done) | copy-start | bytes 6291460
  238.6 1.5 copy-start.3
  242.7 212.9 %reduce-scatter.3.cloned.1.call-start = ((), (), s32[]{:S(2)}) async-start(), calls=%async_computation.5 | async-start | bytes 2162688 | tf_op jit(solution)/shard_map/reduce_scatter | solution.py:39
  248.5 101.4 %copy-start.5 = (f32[32,64]{1,0:T(8,128)S(1)}, f32[32,64]{1,0:T(8,128)}, u32[]{:S(2)}) copy-start(f32[32,64]{1,0:T(8,128)} %param.15) | copy-start | bytes 24580
  248.5 207.1 %copy-start.4 = (f32[32,512]{1,0:T(8,128)S(1)}, f32[32,512]{1,0:T(8,128)}, u32[]{:S(2)}) copy-start(f32[32,512]{1,0:T(8,128)} %param.14) | copy-start | bytes 196612
Sparse Core Ops, SparseCore 0:
  36.0 78.6 all-gather.3
  116.8 70.5 all-gather.5
  190.5 55.6 all-gather.7
  250.3 99.5 reduce-scatter.4
  354.2 101.3 reduce-scatter.2
where the time goes:
time: 465 us; the launch traced here: 464 us
  waiting for transfers between devices  278 us (60%)
  other arithmetic  86.2 us (19%)
  matrix products  30.8 us (7%)
  blocking collectives  27.8 us (6%)
  local copies, waits for them, and re-layouts  25.9 us (6%)
  between operations  14.2 us (3%)
    reduce_scatter x1, waiting for transfers between devices, local(): lax.psum_scatter(jnp.einsum('rk,rc->kc', picked, left_factor, precision=h...  104 us
    reduce_scatter x1, waiting for transfers between devices, local(): lax.psum_scatter(jnp.einsum('rk,rc->kc', picked, panel_factor, precision=...  95.1 us
    another operation x3, other arithmetic, right_solve(): jax.scipy.linalg.solve_triangular(tile, source.T, trans='T', lower=True)  83.4 us
    all_gather x1, waiting for transfers between devices, local(): whole_diag = lax.all_gather(column_block, 'col', axis=1, tiled=True)  77.2 us
    all_gather x1, blocking collectives, local(): column_block = lax.all_gather(diag_factor, 'row', axis=0, tiled=True)  27.8 us
    another operation x40, local copies, waits for them, and re-layouts  23.8 us
    another operation x15, matrix products, right_solve(): jax.scipy.linalg.solve_triangular(tile, source.T, trans='T', lower=True)  17.1 us
  transfers between devices with their start and end apart: 5, of which 3 were waited for; matrix products, arithmetic and copies ran while one was open for 30% of the time, Pallas kernels for 0%

commit v1 on v0

--- a/solution.py
+++ b/solution.py
@@ -22,7 +22,8 @@
     block_width = panel_adjoint.shape[1]
     my_col = lax.axis_index("col")
     my_row = lax.axis_index("row")
-    column_block = lax.all_gather(diag_factor, "row", axis=0, tiled=True)
+    copies = jnp.concatenate([diag_factor] * lax.axis_size("row"), axis=0)
+    column_block = lax.all_to_all(copies, "row", 0, 0, tiled=True)
     whole_diag = lax.all_gather(column_block, "col", axis=1, tiled=True)
     full_rows = lax.all_gather(panel_adjoint, "col", axis=1, tiled=True)
     solved = right_solve(whole_diag, full_rows)

time: 465 us -> 481 us (1.034)
  local copies, waits for them, and re-layouts: 25.9 us -> 50 us
  blocking collectives: 27.8 us -> 16.4 us
    all_gather x1 -> x0, blocking collectives: 27.8 us -> none  [local(): column_block = lax.all_gather(diag_factor, 'row', axis=0, tiled=True)]
    unnamed x30 -> x63, local copies, waits for them, and re-layouts: 0.39 us -> 23.3 us
    all_to_all x0 -> x1, blocking collectives: none -> 16.4 us  [local(): column_block = lax.all_to_all(copies, 'row', 0, 0, tiled=True)]
  transfers between devices with their start and end apart: 5 -> 5, of which waited for: 3 -> 3; matrix products, arithmetic and copies ran while one was open for 30% -> 29% of each run, Pallas kernels for 0% -> 0%
where the time goes in v1:
time: 481 us; the launch traced here: 478 us
  waiting for transfers between devices  279 us (58%)
  other arithmetic  87.5 us (18%)
  local copies, waits for them, and re-layouts  50 us (10%)
  matrix products  30.8 us (6%)
  blocking collectives  16.4 us (3%)
  between operations  14.2 us (3%)
    reduce_scatter x1, waiting for transfers between devices, local(): lax.psum_scatter(jnp.einsum('rk,rc->kc', picked, left_factor, precision=h...  104 us
    reduce_scatter x1, waiting for transfers between devices, local(): lax.psum_scatter(jnp.einsum('rk,rc->kc', picked, panel_factor, precision=...  95.3 us
    another operation x3, other arithmetic, right_solve(): jax.scipy.linalg.solve_triangular(tile, source.T, trans='T', lower=True)  83.4 us
    all_gather x1, waiting for transfers between devices, local(): whole_diag = lax.all_gather(column_block, 'col', axis=1, tiled=True)  77.9 us
    another operation x40, local copies, waits for them, and re-layouts  23.8 us
    unnamed x63, local copies, waits for them, and re-layouts  23.3 us
    another operation x15, matrix products, right_solve(): jax.scipy.linalg.solve_triangular(tile, source.T, trans='T', lower=True)  17.1 us
    all_to_all x1, blocking collectives, local(): column_block = lax.all_to_all(copies, 'row', 0, 0, tiled=True)  16.4 us
  transfers between devices with their start and end apart: 5, of which 3 were waited for; matrix products, arithmetic and copies ran while one was open for 29% of the time, Pallas kernels for 0%

profile of v1, /device:TPU:2, one launch (start us, length us, event | category | flops | bytes accessed | tf_op | source)
XLA Modules:
  0.0 478.5 jit_solution(5396131247782912949)
XLA Ops:
  7.2 0.8 constant_dynamic-update-slice_fusion.31
  8.0 0.7 constant_dynamic-update-slice_fusion.30
  8.7 0.7 constant_dynamic-update-slice_fusion.29
  9.5 0.7 constant_dynamic-update-slice_fusion.28
  10.2 0.7 constant_dynamic-update-slice_fusion.27
  10.9 0.7 constant_dynamic-update-slice_fusion.26
  11.6 0.7 constant_dynamic-update-slice_fusion.25
  12.3 0.7 constant_dynamic-update-slice_fusion.24
  13.1 0.7 constant_dynamic-update-slice_fusion.23
  13.8 0.7 constant_dynamic-update-slice_fusion.22
  14.5 0.7 constant_dynamic-update-slice_fusion.21
  15.2 0.7 constant_dynamic-update-slice_fusion.20
  15.9 0.7 constant_dynamic-update-slice_fusion.19
  16.7 0.7 constant_dynamic-update-slice_fusion.18
  17.4 0.7 constant_dynamic-update-slice_fusion.17
  18.1 0.7 constant_dynamic-update-slice_fusion.16
  28.9 0.7 constant_dynamic-update-slice_fusion.1
  30.6 16.4 %all_to_all.12 = f32[32,1,2048]{2,1,0:T(1,128)S(1)} all-to-all(f32[32,1,2048]{2,1,0:T(1,128)S(1)} %reshape.53), channel_id=1, replica_groups=mesh['row'=32,'col'=16] {'row'}, dimensions={0} | all-to-all | bytes 524288 | tf_op jit(solution)/shard_map/all_to_all | solution.py:26
  47.5 1.3 reduce
  49.0 0.9 copy.14
  51.5 77.9 %all-gather.4.cloned.1.call-done = f32[1024,1024]{0,1:T(8,128)} async-done(((f32[1024,64]{0,1:T(8,128)}), f32[1024,1024]{0,1:T(8,128)}) %all-gather.4.cloned.1.call-update) | async-done | bytes 4194320 | tf_op jit(solution)/shard_map/all_gather | solution.py:27
  129.4 4.8 fusion
  134.2 24.1 %while.1 = (s32[]{:T(128)}, f32[1024,1024]{0,1:T(8,128)}, s32[8,2]{0,1:T(2,128)S(1)}, f32[8,128,128]{2,1,0:T(8,128)S(1)}, s32[]{:T(128)}) while((s32[]{:T(128)}, f32[1024,1024]{0,1:T(8,128)}, s32[8,2]{0,1:T(2,128)S(1)}, f32[8,128,128]{2,1,0:T(8,128)S(1)}, s32[]{:T(128)}) %tuple.28), condition=%wide.while_cond, body=%wide.while_body.sunk | while | flops 2 | bytes 393321 | solution.py:8
  134.8 2.3 dynamic-slice.12
  137.8 2.3 dynamic-slice.12
  140.8 2.3 dynamic-slice.12
  143.8 2.3 dynamic-slice.12
  146.9 2.3 dynamic-slice.12
  149.9 2.3 dynamic-slice.12
  152.9 2.3 dynamic-slice.12
  155.9 2.2 dynamic-slice.12
  158.3 78.6 %custom-call.4 = f32[8,128,128]{1,2,0:T(8,128)S(1)} custom-call(f32[8,128,128]{2,1,0:T(8,128)S(1)} %get-tuple-element.11), custom_call_target="InvertDiagBlocksLowerTriangular" | custom-call | tf_op jit(solution)/shard_map/jit(_solve_triangular)/triangular_solve | solution.py:8
  236.9 1.5 fusion.19
  238.5 1.4 convolution_subtract_fusion.4
  240.2 1.4 convolution_subtract_fusion.3
  242.0 1.6 convolution_subtract_fusion.6
  244.0 1.7 convolution_subtract_fusion.7
  246.1 1.9 convolution_subtract_fusion.2
  248.5 2.0 convolution_subtract_fusion.5
  251.1 2.2 convolution_subtract_fusion.1
  253.4 1.2 convolution_dynamic-update-slice_fusion
  254.8 2.6 fusion.36
  257.7 4.8 %fusion.35 = f32[1024,512]{1,0:T(8,128)} fusion(f32[1024,512]{1,0:T(8,128)S(1)} %constant_dynamic-update-slice_fusion.50, f32[512,512]{1,0:T(8,128)S(1)} %copy-done), kind=kOutput, calls=%fused_computation.117 | convolution fusion | flops 3221225472 | bytes 5242880 | tf_op jit(solution)/shard_map/rk,rc->kc/dot_general | solution.py:41
  263.2 6.4 %convolution_subtract_fusion = f32[512,512]{1,0:T(8,128)} fusion(f32[512,512]{1,0:T(8,128)} %param.13, f32[1024,512]{1,0:T(8,128)S(1)} %constant_dynamic-update-slice_fusion.50, f32[1024,512]{1,0:T(8,128)} %all-gather.8.cloned.1.call-done), kind=kOutput, calls=%fused_computation.4 | convolution fusion | flops 3221487616 | bytes 6291456 | tf_op jit(solution)/shard_map/dot_general | solution.py:32
  269.6 95.3 %reduce-scatter.5.cloned.1.call-done = f32[32,64]{1,0:T(8,128)} async-done(((f32[1024,64]{1,0:T(8,128)}), f32[32,64]{1,0:T(8,128)}) %reduce-scatter.5.cloned.1.call-update) | async-done | bytes 8208 | tf_op jit(solution)/shard_map/reduce_scatter | solution.py:47
  364.9 1.4 select_subtract_fusion
  366.3 104.2 %reduce-scatter.3.cloned.1.call-done = f32[32,512]{1,0:T(8,128)} async-done(((f32[1024,512]{1,0:T(8,128)}), f32[32,512]{1,0:T(8,128)}) %reduce-scatter.3.cloned.1.call-update) | async-done | bytes 65552 | tf_op jit(solution)/shard_map/reduce_scatter | solution.py:40
  470.5 1.5 sub.10
  (108 shorter events, 22.6 us)
Async XLA Ops:
  7.2 250.5 %copy-start = (f32[512,512]{1,0:T(8,128)S(1)}, f32[512,512]{1,0:T(8,128)}, u32[]{:S(2)}) copy-start(f32[512,512]{1,0:T(8,128)} %param.10) | copy-start | bytes 3145732
  7.2 122.2 %all-gather.4.cloned.1.call-start = ((), (), s32[]{:S(2)}) async-start(), calls=%async_computation.3 | async-start | bytes 4456448 | tf_op jit(solution)/shard_map/all_gather | solution.py:27
  49.9 187.0 %all-gather.6.cloned.1.call-start = ((), (), s32[]{:S(2)}) async-start(), calls=%async_computation.4 | async-start | bytes 2228224 | tf_op jit(solution)/shard_map/all_gather | solution.py:28
  50.7 212.5 %all-gather.8.cloned.1.call-start = ((), (), s32[]{:S(2)}) async-start(), calls=%async_computation.5 | async-start | bytes 2162688 | tf_op jit(solution)/shard_map/all_gather | solution.py:34
  51.4 313.5 %reduce-scatter.5.cloned.1.call-start = ((), (), s32[]{:S(2)}) async-start(), calls=%async_computation.7 | async-start | bytes 540672 | tf_op jit(solution)/shard_map/reduce_scatter | solution.py:47
  236.9 13.7 %copy-start.2 = (f32[8,128,128]{1,2,0:T(8,128)}, f32[8,128,128]{1,2,0:T(8,128)S(1)}, u32[]{:S(2)}) copy-start(f32[8,128,128]{1,2,0:T(8,128)S(1)} %custom-call.4) | copy-start | bytes 1572868
  236.9 5.1 %copy-start.1 = (f32[512,1024]{0,1:T(8,128)S(1)}, f32[512,1024]{0,1:T(8,128)}, u32[]{:S(2)}) copy-start(f32[512,1024]{0,1:T(8,128)} %all-gather.6.cloned.1.call-done) | copy-start | bytes 6291460
  253.3 1.5 copy-start.3
  257.4 213.0 %reduce-scatter.3.cloned.1.call-start = ((), (), s32[]{:S(2)}) async-start(), calls=%async_computation.6 | async-start | bytes 2162688 | tf_op jit(solution)/shard_map/reduce_scatter | solution.py:40
  263.2 101.7 %copy-start.5 = (f32[32,64]{1,0:T(8,128)S(1)}, f32[32,64]{1,0:T(8,128)}, u32[]{:S(2)}) copy-start(f32[32,64]{1,0:T(8,128)} %param.15) | copy-start | bytes 24580
  263.2 207.2 %copy-start.4 = (f32[32,512]{1,0:T(8,128)S(1)}, f32[32,512]{1,0:T(8,128)}, u32[]{:S(2)}) copy-start(f32[32,512]{1,0:T(8,128)} %param.14) | copy-start | bytes 196612
Sparse Core Ops, SparseCore 0:
  50.1 79.2 all-gather.3
  131.5 70.2 all-gather.5
  204.9 56.1 all-gather.7
  265.3 99.5 reduce-scatter.4
  369.1 101.2 reduce-scatter.2
